TPU v7x, 256 devices: a whole 4x4x8 slice. The times are simulated.
256 devices in a mesh: row: 8 (over z), col: 16 (over x, y), rep: 2 (over core).
Axes of the slice: x: 4, y: 4, z: 8, core: 2. Of those that a mesh axis runs over, the one named last changes fastest.
Arguments:
- features: bfloat16 [65536, 256], P(('row', 'col', 'rep')), may hold values from -6 to 6
- tile_values: bfloat16 [8, 16, 2, 192, 128, 128], P('row', 'col', 'rep'), may hold values from -0.0546875 to 0.0546875
- tile_row: int32 [8, 16, 2, 192], P('row', 'col', 'rep'), may hold values from 0 to 63
- tile_col: int32 [8, 16, 2, 192], P('row', 'col', 'rep'), may hold values from 0 to 31
- tile_count: int32 [8, 16, 2], P('row', 'col', 'rep'), may hold values from 48 to 192, as said below
- weight: bfloat16 [256, 172], replicated, may hold values from -0.375 to 0.375
- labels: int32 [65536], P(('row', 'col', 'rep')), may hold values from 0 to 171
Outputs:
- logits: float32 [65536, 172], P(('row', 'col', 'rep'))
- grad_features: float32 [65536, 256], P(('row', 'col', 'rep'))
- grad_weight: float32 [256, 172], replicated
Inputs may be any that keep to these rules, and one draw needn't show every extreme that they name: `tile_count`: slots at or beyond a device's count hold values that take no part. At least a quarter of every device's slots are live, and some device has all 192 live in every draw.
All inputs are finite; a program needn't handle non-finite values.
Results may differ from a plain program's by a relative error of at most 0.0095.
Values may be sent and summed in bfloat16 or wider, within the bound.
A program may use at most 128 MiB of HBM per device.

v0:
```python
import jax
import jax.numpy as jnp
from jax import lax
from jax.sharding import PartitionSpec as P


def block_product(values, take_ids, put_ids, count, source, acc, backward):
    group = 32
    turns = (count + group - 1) // group

    def step(turn, total):
        start = turn * group
        part = lax.dynamic_slice_in_dim(values, start, group, 0)
        take = lax.dynamic_slice_in_dim(take_ids, start, group, 0)
        put = lax.dynamic_slice_in_dim(put_ids, start, group, 0)
        alive = start + jnp.arange(group, dtype=jnp.int32) < count
        picked = jnp.take(source, take, axis=0)
        if backward:
            prod = jnp.einsum("gji,gjw->giw", part, picked, preferred_element_type=jnp.float32)
        else:
            prod = jnp.einsum("gij,gjw->giw", part, picked, preferred_element_type=jnp.float32)
        prod = jnp.where(alive[:, None, None], prod, 0.0)
        return total.at[put].add(prod)

    return lax.fori_loop(0, turns, step, acc)


def local(features, tile_values, tile_row, tile_col, tile_count, weight, labels):
    tile = tile_values.shape[-1]
    slots = tile_values.shape[3]
    width = features.shape[1]
    classes = weight.shape[1]
    own_rows = features.shape[0]
    n_row = lax.axis_size("row")
    n_col = lax.axis_size("col")
    n_rep = lax.axis_size("rep")
    row_blocks = n_col * n_rep * own_rows // tile
    col_blocks = n_row * n_rep * own_rows // tile
    values = tile_values.reshape(slots, tile, tile)
    block_rows = tile_row.reshape(slots)
    block_cols = tile_col.reshape(slots)
    count = tile_count.reshape(())
    panel = lax.all_gather(features, ("row", "rep"), axis=0, tiled=True).reshape(
        col_blocks, tile, width
    )
    jobs = ((values, block_rows, block_cols, count),)
    partial_value = jnp.zeros((row_blocks, tile, width), jnp.float32)
    job = jobs[0]
    partial_value = block_product(job[0], job[2], job[1], job[3], panel, partial_value, False)
    hidden = lax.psum_scatter(
        partial_value.reshape(row_blocks * tile, width),
        ("col", "rep"),
        scatter_dimension=0,
        tiled=True,
    )
    hidden = hidden.astype(jnp.bfloat16)
    logits = jnp.dot(hidden, weight, preferred_element_type=jnp.float32)
    expos = jnp.exp(logits)
    prob = expos / jnp.sum(expos, axis=1, keepdims=True)
    onehot = (labels[:, None] == jnp.arange(classes, dtype=jnp.int32)[None, :]).astype(jnp.float32)
    grad_logits = (prob - onehot).astype(jnp.bfloat16)
    grad_hidden = jnp.dot(grad_logits, weight.T, preferred_element_type=jnp.float32).astype(
        jnp.bfloat16
    )
    grad_weight = lax.psum(
        jnp.dot(hidden.T, grad_logits, preferred_element_type=jnp.float32), ("row", "col", "rep")
    )
    row_panel = lax.all_gather(grad_hidden, ("col", "rep"), axis=0, tiled=True).reshape(
        row_blocks, tile, width
    )
    back = jnp.zeros((col_blocks, tile, width), jnp.float32)
    job = jobs[0]
    back = block_product(job[0], job[1], job[2], job[3], row_panel, back, True)
    grad_features = lax.psum_scatter(
        back.reshape(col_blocks * tile, width), ("row", "rep"), scatter_dimension=0, tiled=True
    )
    return (logits, grad_features, grad_weight)


def solution(mesh):
    in_specs = (
        P(("row", "col", "rep"), None),
        P("row", "col", "rep", None, None, None),
        P("row", "col", "rep", None),
        P("row", "col", "rep", None),
        P("row", "col", "rep"),
        P(),
        P(("row", "col", "rep")),
    )
    out_specs = (P(("row", "col", "rep"), None), P(("row", "col", "rep"), None), P())
    return jax.shard_map(local, mesh=mesh, in_specs=in_specs, out_specs=out_specs, check_vma=False)
```

profile of v0, /device:TPU:8, one launch (start us, length us, event | category | flops | bytes accessed | tf_op | source)
XLA Modules:
  0.0 636.1 jit_solution(364267122824797924)
XLA Ops:
  7.2 0.7 all-gather.3.cloned.1.call-update
  8.6 43.9 %all-gather.3.cloned.1.call-done = bf16[4096,256]{1,0:T(8,128)(2,1)} async-done(((bf16[256,256]{1,0:T(8,128)(2,1)}), bf16[4096,256]{1,0:T(8,128)(2,1)}) %all-gather.3.cloned.1.call-update) | async-done | bytes 2097168 | tf_op jit(solution)/shard_map/all_gather | solution.py:43
  52.5 4.3 broadcast_in_dim.61
  56.8 68.5 %while.20 = (s32[]{:T(128)}, f32[64,128,256]{2,1,0:T(8,128)}, s32[]{:T(128)}, s32[192]{0:T(256)S(1)}, s32[]{:T(128)}, /*index=5*/bf16[192,128,128]{2,1,0:T(8,128...) while((s32[]{:T(128)}, f32[64,128,256]{2,1,0:T(8,128)}, ...), condition=%wide.region_2.3_spmd, body=%wide.region_0.2_spmd.sunk | while | flops 271582560 | bytes 24122552 | solution.py:25
  56.8 0.7 compare_and_fusion.4
  57.5 2.3 gather_fusion
  59.8 4.0 convolution_select_fusion.4
  63.8 10.1 %scatter_fusion = f32[64,128,256]{2,1,0:T(8,128)} fusion(f32[64,128,256]{2,1,0:T(8,128)} %get-tuple-element.264, s32[32]{0:T(128)S(1)} %compare_select_fusion.8, f32[32,128,256]{2,1,0:T(8,128)} %convolution_select_fusion.4), kind=kCustom, calls=%fused_computation.2.clone.1 | custom fusion | flops 1048576 | bytes 12583040 | tf_op jit(solution)/shard_map/while/body/scatter-add | solution.py:23
  74.0 0.7 compare_and_fusion.4
  74.7 2.3 gather_fusion
  77.0 4.0 convolution_select_fusion.4
  81.0 10.0 %scatter_fusion = f32[64,128,256]{2,1,0:T(8,128)} fusion(f32[64,128,256]{2,1,0:T(8,128)} %get-tuple-element.264, s32[32]{0:T(128)S(1)} %compare_select_fusion.8, f32[32,128,256]{2,1,0:T(8,128)} %convolution_select_fusion.4), kind=kCustom, calls=%fused_computation.2.clone.1 | custom fusion | flops 1048576 | bytes 12583040 | tf_op jit(solution)/shard_map/while/body/scatter-add | solution.py:23
  91.0 0.7 compare_and_fusion.4
  91.8 2.3 gather_fusion
  94.0 4.0 convolution_select_fusion.4
  98.0 0.1 compare_select_fusion.8
  98.1 10.1 %scatter_fusion = f32[64,128,256]{2,1,0:T(8,128)} fusion(f32[64,128,256]{2,1,0:T(8,128)} %get-tuple-element.264, s32[32]{0:T(128)S(1)} %compare_select_fusion.8, f32[32,128,256]{2,1,0:T(8,128)} %convolution_select_fusion.4), kind=kCustom, calls=%fused_computation.2.clone.1 | custom fusion | flops 1048576 | bytes 12583040 | tf_op jit(solution)/shard_map/while/body/scatter-add | solution.py:23
  108.1 0.7 compare_and_fusion.4
  108.9 2.3 gather_fusion
  111.2 4.0 convolution_select_fusion.4
  115.2 10.1 %scatter_fusion = f32[64,128,256]{2,1,0:T(8,128)} fusion(f32[64,128,256]{2,1,0:T(8,128)} %get-tuple-element.264, s32[32]{0:T(128)S(1)} %compare_select_fusion.8, f32[32,128,256]{2,1,0:T(8,128)} %convolution_select_fusion.4), kind=kCustom, calls=%fused_computation.2.clone.1 | custom fusion | flops 1048576 | bytes 12583040 | tf_op jit(solution)/shard_map/while/body/scatter-add | solution.py:23
  125.3 132.6 %reduce-scatter.3.cloned.1.call-done = f32[256,256]{1,0:T(8,128)} async-done(((f32[8192,256]{1,0:T(8,128)}), f32[256,256]{1,0:T(8,128)}) %reduce-scatter.3.cloned.1.call-update) | async-done | bytes 262160 | tf_op jit(solution)/shard_map/reduce_scatter | solution.py:50
  258.0 1.2 exponential_reduce_fusion
  259.2 0.9 convolution_convert_fusion
  260.2 8.7 %copy.10 = bf16[1,1,1,192,128,128]{4,5,3,2,1,0:T(8,128)(2,1)} copy(bf16[1,1,1,192,128,128]{5,4,3,2,1,0:T(8,128)(2,1)} %bitcast.17) | data formatting | bytes 12582912 | tf_op args[1]
  268.9 0.9 fusion.12
  269.8 42.2 %all-gather.5.cloned.1.call-done = bf16[8192,256]{1,0:T(8,128)(2,1)} async-done(((bf16[256,256]{1,0:T(8,128)(2,1)}), bf16[8192,256]{1,0:T(8,128)(2,1)}) %all-gather.5.cloned.1.call-update) | async-done | bytes 4194320 | tf_op jit(solution)/shard_map/all_gather | solution.py:68
  312.0 2.5 broadcast_in_dim.62
  314.5 70.4 %while.21 = (s32[]{:T(128)}, f32[32,128,256]{2,1,0:T(8,128)}, s32[]{:T(128)}, s32[192]{0:T(256)S(1)}, s32[]{:T(128)}, /*index=5*/bf16[192,128,128]{1,2,0:T(8,128...) while((s32[]{:T(128)}, f32[32,128,256]{2,1,0:T(8,128)}, ...), condition=%wide.region_7.8_spmd, body=%wide.region_5.7_spmd.sunk | while | flops 271582560 | bytes 24122552 | solution.py:25
  314.5 0.7 compare_and_fusion.5
  315.2 2.9 gather_fusion.1
  318.1 4.0 convolution_select_fusion.5
  322.2 9.9 %scatter_fusion.1 = f32[32,128,256]{2,1,0:T(8,128)} fusion(f32[32,128,256]{2,1,0:T(8,128)} %get-tuple-element.300, s32[32]{0:T(128)S(1)} %compare_select_fusion.9, f32[32,128,256]{2,1,0:T(8,128)} %convolution_select_fusion.5), kind=kCustom, calls=%fused_computation.3.clone.1 | custom fusion | flops 1048576 | bytes 12583040 | tf_op jit(solution)/shard_map/while/body/scatter-add | solution.py:23
  332.1 0.7 compare_and_fusion.5
  332.8 2.9 gather_fusion.1
  335.7 4.0 convolution_select_fusion.5
  339.8 9.9 %scatter_fusion.1 = f32[32,128,256]{2,1,0:T(8,128)} fusion(f32[32,128,256]{2,1,0:T(8,128)} %get-tuple-element.300, s32[32]{0:T(128)S(1)} %compare_select_fusion.9, f32[32,128,256]{2,1,0:T(8,128)} %convolution_select_fusion.5), kind=kCustom, calls=%fused_computation.3.clone.1 | custom fusion | flops 1048576 | bytes 12583040 | tf_op jit(solution)/shard_map/while/body/scatter-add | solution.py:23
  349.6 0.7 compare_and_fusion.5
  350.4 2.9 gather_fusion.1
  353.3 4.0 convolution_select_fusion.5
  357.3 10.0 %scatter_fusion.1 = f32[32,128,256]{2,1,0:T(8,128)} fusion(f32[32,128,256]{2,1,0:T(8,128)} %get-tuple-element.300, s32[32]{0:T(128)S(1)} %compare_select_fusion.9, f32[32,128,256]{2,1,0:T(8,128)} %convolution_select_fusion.5), kind=kCustom, calls=%fused_computation.3.clone.1 | custom fusion | flops 1048576 | bytes 12583040 | tf_op jit(solution)/shard_map/while/body/scatter-add | solution.py:23
  367.4 0.7 compare_and_fusion.5
  368.1 2.9 gather_fusion.1
  371.0 4.0 convolution_select_fusion.5
  375.1 9.8 %scatter_fusion.1 = f32[32,128,256]{2,1,0:T(8,128)} fusion(f32[32,128,256]{2,1,0:T(8,128)} %get-tuple-element.300, s32[32]{0:T(128)S(1)} %compare_select_fusion.9, f32[32,128,256]{2,1,0:T(8,128)} %convolution_select_fusion.5), kind=kCustom, calls=%fused_computation.3.clone.1 | custom fusion | flops 1048576 | bytes 12583040 | tf_op jit(solution)/shard_map/while/body/scatter-add | solution.py:23
  384.9 178.5 %all-reduce.2.cloned.1.call-done = f32[256,172]{0,1:T(8,128)} async-done(((f32[256,172]{0,1:T(8,128)}), f32[256,172]{0,1:T(8,128)}) %all-reduce.2.cloned.1.call-update) | async-done | bytes 176144 | tf_op jit(solution)/shard_map/psum | solution.py:65
  563.4 64.5 %reduce-scatter.5.cloned.1.call-done = f32[256,256]{1,0:T(8,128)} async-done(((f32[4096,256]{1,0:T(8,128)}), f32[256,256]{1,0:T(8,128)}) %reduce-scatter.5.cloned.1.call-update) | async-done | bytes 262160 | tf_op jit(solution)/shard_map/reduce_scatter | solution.py:74
  628.0 1.6 copy.29
  (36 shorter events, 0.9 us)
Async XLA Ops:
  7.2 250.8 %copy-start = (bf16[256,172]{0,1:T(8,128)(2,1)S(1)}, bf16[256,172]{0,1:T(8,128)(2,1)}, u32[]{:S(2)}) copy-start(bf16[256,172]{0,1:T(8,128)(2,1)} %param.16) | copy-start | bytes 264196
  7.2 45.3 %all-gather.3.cloned.1.call-start = ((), (), s32[]{:S(2)}) async-start(), calls=%async_computation.2 | async-start | bytes 2228224 | tf_op jit(solution)/shard_map/all_gather | solution.py:43
  7.9 250.1 %reduce-scatter.3.cloned.1.call-start = ((), (), s32[]{:S(2)}) async-start(), calls=%async_computation.3 | async-start | bytes 8650752 | tf_op jit(solution)/shard_map/reduce_scatter | solution.py:50
  52.5 4.3 copy-start.3
  52.5 4.3 copy-start.4
  125.3 133.9 %copy-start.5 = (s32[256]{0:T(256)S(1)}, s32[256]{0:T(256)}, u32[]{:S(2)}) copy-start(s32[256]{0:T(256)} %param.17) | copy-start | bytes 3076
  125.3 186.7 %all-gather.5.cloned.1.call-start = ((), (), s32[]{:S(2)}) async-start(), calls=%async_computation.4 | async-start | bytes 4325376 | tf_op jit(solution)/shard_map/all_gather | solution.py:68
  259.2 9.7 %copy-start.2 = (f32[256,172]{0,1:T(8,128)}, f32[256,172]{0,1:T(8,128)S(1)}, u32[]{:S(2)}) copy-start(f32[256,172]{0,1:T(8,128)S(1)} %get-tuple-element.323) | copy-start | bytes 528388
  260.1 8.7 %copy-start.1 = (f32[256,256]{1,0:T(8,128)S(1)}, f32[256,256]{1,0:T(8,128)}, u32[]{:S(2)}) copy-start(f32[256,256]{1,0:T(8,128)} %reduce-scatter.3.cloned.1.call-done) | copy-start | bytes 786436
  260.1 303.3 %all-reduce.2.cloned.1.call-start = ((), (), s32[]{:S(2)}) async-start(), calls=%async_computation.6 | async-start | bytes 360448 | tf_op jit(solution)/shard_map/psum | solution.py:65
  269.7 358.2 %reduce-scatter.5.cloned.1.call-start = ((), (), s32[]{:S(2)}) async-start(), calls=%async_computation.5 | async-start | bytes 4456448 | tf_op jit(solution)/shard_map/reduce_scatter | solution.py:74
Sparse Core Ops, SparseCore 0:
  9.8 42.6 all-gather.2
  125.4 132.5 reduce-scatter.2
  261.4 50.4 all-gather.4
  318.8 244.5 all-reduce.1
  566.5 61.3 reduce-scatter.4
where the time goes:
time: 637 us; the launch traced here: 636 us
  waiting for transfers between devices  462 us (73%)
  other arithmetic  86.3 us (14%)
  local copies, waits for them, and re-layouts  37.7 us (6%)
  matrix products  34.8 us (5%)
  between operations  14.5 us (2%)
    psum x1, waiting for transfers between devices, local(): lax.psum(jnp.dot(hidden.T, grad_logits, preferred_element_type=jnp.float3...  178 us
    reduce_scatter x1, waiting for transfers between devices, local(): lax.psum_scatter(partial_value.reshape(row_blocks * tile, width), ('col',...  133 us
    scatter-add x8, other arithmetic, step(): return total.at[put].add(prod)  79.9 us
    reduce_scatter x1, waiting for transfers between devices, local(): lax.psum_scatter(back.reshape(col_blocks * tile, width), ('row', 'rep'),...  64.5 us
    all_gather x1, waiting for transfers between devices, local(): lax.all_gather(features, ('row', 'rep'), axis=0, tiled=True)  43.9 us
    all_gather x1, waiting for transfers between devices, local(): lax.all_gather(grad_hidden, ('col', 'rep'), axis=0, tiled=True)  42.2 us
    gather x8, local copies, waits for them, and re-layouts, step(): picked = jnp.take(source, take, axis=0)  20.6 us
    dot_general x4, matrix products, step(): jnp.einsum('gji,gjw->giw', part, picked, preferred_element_type=jnp.float32)  16 us
  transfers between devices with their start and end apart: 5, of which 5 were waited for; matrix products, arithmetic and copies ran while one was open for 13% of the time, Pallas kernels for 0%

commit v1 on v0

v1 whole, which is shorter than its diff:
```python
import functools

import jax
import jax.numpy as jnp
from jax import lax
from jax.experimental import pallas as pl
from jax.experimental.pallas import tpu as pltpu
from jax.sharding import PartitionSpec as P

BF = jnp.bfloat16
F32 = jnp.float32
VM = pltpu.VMEM
SIDE = 4
GROUP = 16
UNROLL = 4


class Link:
    def __init__(self, send, recv):
        self.send, self.recv, self.used, self.live = send, recv, 0, []

    def slot(self):
        self.used += 1
        return self.used - 1

    def start(self, src, dst, device, slot):
        copy = pltpu.make_async_remote_copy(
            src_ref=src,
            dst_ref=dst,
            send_sem=self.send.at[slot],
            recv_sem=self.recv.at[slot],
            device_id=device,
            device_id_type=pl.DeviceIdType.MESH,
        )
        copy.start()
        self.live.append(copy)

    def arrived(self, dst, slot):
        pltpu.make_async_remote_copy(
            src_ref=dst,
            dst_ref=dst,
            send_sem=self.send.at[slot],
            recv_sem=self.recv.at[slot],
            device_id={"rep": 1 - lax.axis_index("rep")},
            device_id_type=pl.DeviceIdType.MESH,
        ).wait_recv()

    def drain(self):
        for copy in self.live:
            copy.wait_send()


def enter(devices):
    barrier = pltpu.get_barrier_semaphore()
    for device in devices:
        pl.semaphore_signal(
            barrier, inc=1, device_id=device, device_id_type=pl.DeviceIdType.MESH
        )
    pl.semaphore_wait(barrier, len(devices))


def gather_z(feat, panel, send, recv):
    r, p = lax.axis_index("row"), lax.axis_index("rep")
    n = panel.shape[0]
    at = lambda k: lax.rem(r + k + 2 * n, n)
    right, left, twin = {"row": at(1)}, {"row": at(-1)}, {"rep": 1 - p}
    enter((right, left, twin))
    link = Link(send, recv)
    subs, rows = 2, feat.shape[0] // 2
    own = [feat.at[pl.ds(j * rows, rows)] for j in range(subs)]
    slot = {}
    for j in range(subs):
        for d, dev in ((1, right), (-1, left)):
            slot[1, d, j] = link.slot()
            link.start(own[j], panel.at[r, p, pl.ds(j * rows, rows)], dev, slot[1, d, j])
    slot["own"] = link.slot()
    link.start(feat, panel.at[r, p], twin, slot["own"])
    panel[r, p] = feat[...]
    twins = [(panel.at[r, 1 - p], slot["own"])]
    half = n // 2
    for k in range(1, half + 1):
        for j in range(subs):
            for d, dev in ((1, right), (-1, left)):
                if k == half and (j == 0) != (d == 1):
                    continue
                part = panel.at[at(-k * d), p, pl.ds(j * rows, rows)]
                link.arrived(part, slot[k, d, j])
                if k + 1 < half or (k + 1 == half and (j == 0) == (d == 1)):
                    slot[k + 1, d, j] = link.slot()
                    link.start(part, part, dev, slot[k + 1, d, j])
                extra = link.slot()
                link.start(part, part, twin, extra)
                twins.append((panel.at[at(-k * d), 1 - p, pl.ds(j * rows, rows)], extra))
    for part, extra in twins:
        link.arrived(part, extra)
    link.drain()


def tiles_kernel(backward, take_ids, put_ids, count, tiles, panel, out, acc):
    step = pl.program_id(0)
    base = step * GROUP
    live_count = count[0]

    @pl.when(step == 0)
    def _():
        acc[...] = jnp.zeros_like(acc)

    def body(turn, carry):
        for u in range(UNROLL):
            s = turn * UNROLL + u
            slot = base + s
            source = panel[take_ids[slot]]
            if backward:
                prod = lax.dot_general(
                    tiles[s], source, (((0,), (0,)), ((), ())), preferred_element_type=F32
                )
            else:
                prod = jnp.dot(tiles[s], source, preferred_element_type=F32)
            prod = jnp.where(slot < live_count, prod, 0.0)
            acc[put_ids[slot]] += prod
        return carry

    lax.fori_loop(0, GROUP // UNROLL, body, 0)

    @pl.when(step == pl.num_programs(0) - 1)
    def _():
        out[...] = acc[...].astype(out.dtype)


def multiply(backward, values, take_ids, put_ids, count, panel, blocks):
    slots, tile, _ = values.shape
    width = panel.shape[-1]
    return pl.pallas_call(
        functools.partial(tiles_kernel, backward),
        out_shape=jax.ShapeDtypeStruct((blocks, tile, width), BF),
        grid_spec=pltpu.PrefetchScalarGridSpec(
            num_scalar_prefetch=3,
            grid=(slots // GROUP,),
            in_specs=[
                pl.BlockSpec((GROUP, tile, tile), lambda i, *_: (i, 0, 0)),
                pl.BlockSpec(panel.shape, lambda i, *_: (0, 0, 0)),
            ],
            out_specs=pl.BlockSpec((blocks, tile, width), lambda i, *_: (0, 0, 0)),
            scratch_shapes=[VM((blocks, tile, width), F32)],
        ),
        compiler_params=pltpu.CompilerParams(vmem_limit_bytes=48 * 1024 * 1024),
    )(take_ids, put_ids, count, values, panel)


def add(a, b):
    return (a.astype(F32) + b.astype(F32)).astype(BF)


def plane_kernel(
    part, weight, labels, logits, panel, term,
    summed, far1, near1, mid, far2, near2, hidden, wpad, gw, gw1, gw2, send, recv,
):
    c, p = lax.axis_index("col"), lax.axis_index("rep")
    x, y = c // SIDE, lax.rem(c, SIDE)
    wrap = lambda v: lax.rem(v + 2 * SIDE, SIDE)
    twin = {"rep": 1 - p}
    pos = (x, y)

    def to(axis, k):
        if axis == 0:
            return {"col": wrap(x + k) * SIDE + y}
        return {"col": x * SIDE + wrap(y + k)}

    peers = [{"col": wrap(x + k) * SIDE + y, "rep": lax.rem(p + e, 2)}
             for k in range(SIDE) for e in range(2) if (k, e) != (0, 0)]
    mates = [to(1, k) for k in range(1, SIDE)]
    enter([*peers, *mates])
    link = Link(send, recv)
    rows = panel.shape[3]
    half = rows // 2
    cut = (pl.ds(0, half), pl.ds(half, half))

    def block(ref, h, a, b, *lead):
        if h == 0:
            return ref.at[(a, b, *lead, cut[0])]
        return ref.at[(b, a, *lead, cut[1])]

    whole, low, high = pl.ds(0, SIDE), pl.ds(0, SIDE // 2), pl.ds(SIDE // 2, SIDE // 2)
    order = [(h, k) for k in (2, 1, -1, 0) for h in (0, 1)]
    cores = {}
    for h, k in order:
        cores[h, k] = link.slot()
        a = wrap(pos[h] + k)
        link.start(block(part, h, a, whole, 1 - p), block(summed, h, a, whole), twin, cores[h, k])
    wpad[...] = jnp.zeros_like(wpad)
    classes = weight.shape[1]
    wpad[:, :classes] = weight[...]
    slots = {}

    def first(h, tag, src, dst, k):
        slots[h, tag] = link.slot()
        link.start(src, dst, to(h, k), slots[h, tag])

    for h, k in order:
        a = wrap(pos[h] + k)
        got = block(summed, h, a, whole)
        link.arrived(got, cores[h, k])
        got[...] = add(got[...], block(part, h, a, whole, p)[...])
        if k == 2:
            first(h, "A", block(summed, h, a, low), far1.at[h, 0], 1)
            first(h, "a", block(summed, h, a, high), far1.at[h, 1], -1)
        if k == 1:
            first(h, "B", block(summed, h, a, high), near1.at[h, 0, high], 1)
        if k == -1:
            first(h, "b", block(summed, h, a, low), near1.at[h, 1, low], -1)
            if h == 1:
                for g in (0, 1):
                    for side, tag, k2, span in ((0, "A", 1, low), (1, "a", -1, high)):
                        link.arrived(far1.at[g, side], slots[g, tag])
                        piece = block(summed, g, wrap(pos[g] + k2), span)
                        piece[...] = add(piece[...], far1[g, side])
                        first(g, "C" if side == 0 else "c", piece, near1.at[g, side, span], k2)
    quarter = half // 2
    lo, hi = pl.ds(0, quarter), pl.ds(quarter, quarter)

    def second(h, tag, src, dst, k):
        slots[h, tag] = link.slot()
        link.start(src, dst, to(1 - h, k), slots[h, tag])

    for h in (0, 1):
        link.arrived(near1.at[h, 0, high], slots[h, "B"])
        link.arrived(near1.at[h, 1, low], slots[h, "b"])
        link.arrived(near1.at[h, 0, low], slots[h, "C"])
        link.arrived(near1.at[h, 1, high], slots[h, "c"])
        mine = block(summed, h, pos[h], whole)
        mid[h] = (
            mine[...].astype(F32) + near1[h, 0].astype(F32) + near1[h, 1].astype(F32)
        ).astype(BF)
        o = pos[1 - h]
        second(h, "P", mid.at[h, wrap(o + 2), lo], far2.at[h, 0], 1)
        second(h, "p", mid.at[h, wrap(o + 2), hi], far2.at[h, 1], -1)
        second(h, "Q", mid.at[h, wrap(o + 1), hi], near2.at[h, 0, hi], 1)
        second(h, "q", mid.at[h, wrap(o - 1), lo], near2.at[h, 1, lo], -1)
    for h in (0, 1):
        o = pos[1 - h]
        for side, tag, k, span in ((0, "P", 1, lo), (1, "p", -1, hi)):
            link.arrived(far2.at[h, side], slots[h, tag])
            piece = mid.at[h, wrap(o + k), span]
            piece[...] = add(piece[...], far2[h, side])
            second(h, "R" if side == 0 else "r", piece, near2.at[h, side, span], k)
    nodes = labels.shape[1]
    lanes = wpad.shape[1]
    hot = (
        lax.broadcasted_iota(jnp.int32, (lanes, nodes), 0) == labels[...]
    ).astype(F32).T
    for h in (0, 1):
        link.arrived(near2.at[h, 0, hi], slots[h, "Q"])
        link.arrived(near2.at[h, 1, lo], slots[h, "q"])
        link.arrived(near2.at[h, 0, lo], slots[h, "R"])
        link.arrived(near2.at[h, 1, hi], slots[h, "r"])
        hidden[cut[h]] = (
            mid[h, pos[1 - h]].astype(F32) + near2[h, 0].astype(F32) + near2[h, 1].astype(F32)
        ).astype(BF)

    score = jnp.dot(hidden[...], wpad[...], preferred_element_type=F32)
    logits[...] = score[:, :classes]
    real = lax.broadcasted_iota(jnp.int32, score.shape, 1) < classes
    expos = jnp.where(real, jnp.exp(score), 0.0)
    prob = expos / jnp.sum(expos, axis=1, keepdims=True)
    grad = (prob - hot).astype(BF)
    panel[x, y, p] = lax.dot_general(
        grad, wpad[...], (((1,), (1,)), ((), ())), preferred_element_type=F32
    ).astype(BF)

    twins = []

    def hand(ref_mine, ref_twin):
        slot = link.slot()
        link.start(ref_mine, ref_mine, twin, slot)
        twins.append((ref_twin, slot))

    def spot(h, da, db, core, span=None):
        a, b = wrap(pos[h] + da), wrap(pos[1 - h] + db)
        i, j = (a, b) if h == 0 else (b, a)
        span = span if span is not None else cut[h]
        return panel.at[i, j, core, span]

    quarters = [(pl.ds(h * half, quarter), pl.ds(h * half + quarter, quarter)) for h in (0, 1)]

    def go(key, src, axis, k):
        slots[key] = link.slot()
        link.start(src, src, to(axis, k), slots[key])

    for h in (0, 1):
        own = spot(h, 0, 0, p)
        go((h, "g", 1), own, 1 - h, 1)
        go((h, "g", -1), own, 1 - h, -1)
    for h in (0, 1):
        own = spot(h, 0, 0, p)
        go((h, "s", 1, 0), own, h, 1)
        go((h, "s", -1, 0), own, h, -1)
        hand(own, spot(h, 0, 0, 1 - p))

    gw[...] = lax.dot_general(
        hidden[...], grad, (((0,), (0,)), ((), ())), preferred_element_type=F32
    )
    share = gw.shape[0] // (2 * SIDE)
    slot_w = []
    mine8 = x * 2 + p
    for k in range(SIDE):
        for e in range(2):
            if (k, e) == (0, 0):
                continue
            there = wrap(x + k) * 2 + lax.rem(p + e, 2)
            s = link.slot()
            link.start(gw.at[pl.ds(there * share, share)], gw1.at[mine8],
                       {"col": wrap(x + k) * SIDE + y, "rep": lax.rem(p + e, 2)}, s)
            slot_w.append((gw1.at[wrap(x - k) * 2 + lax.rem(p + e, 2)], s))

    for h in (0, 1):
        for d in (1, -1):
            got = spot(h, 0, -d, p)
            link.arrived(got, slots[h, "g", d])
            q = 0 if d == 1 else 1
            go((h, "f", d), spot(h, 0, -d, p, quarters[h][q]), 1 - h, d)
            go((h, "s", 1, -d), got, h, 1)
            go((h, "s", -1, -d), got, h, -1)
            hand(got, spot(h, 0, -d, 1 - p))

    gw1[mine8] = gw[pl.ds(mine8 * share, share)]
    for ref, s in slot_w:
        link.arrived(ref, s)
    total = gw1[0]
    for i in range(1, 2 * SIDE):
        total += gw1[i]
    gw[pl.ds(mine8 * share, share)] = total
    eighth = share // SIDE
    slot_w = []
    for k in range(1, SIDE):
        there = wrap(y + k)
        s = link.slot()
        link.start(gw.at[pl.ds(mine8 * share + there * eighth, eighth)], gw2.at[y], to(1, k), s)
        slot_w.append((gw2.at[wrap(y - k)], s))
    gw2[y] = gw[pl.ds(mine8 * share + y * eighth, eighth)]

    for h in (0, 1):
        for d in (1, -1):
            q = 0 if d == 1 else 1
            link.arrived(spot(h, 0, 2, p, quarters[h][q]), slots[h, "f", d])
        got = spot(h, 0, 2, p)
        go((h, "s", 1, 2), got, h, 1)
        go((h, "s", -1, 2), got, h, -1)
        hand(got, spot(h, 0, 2, 1 - p))
    for db in (0, 1, -1, 2):
        for h in (0, 1):
            for d in (1, -1):
                got = spot(h, -d, db, p)
                link.arrived(got, slots[h, "s", d, db])
                if (d == 1) == (db in (0, 1)):
                    go((h, "t", db), got, h, d)
                hand(got, spot(h, -d, db, 1 - p))
    for ref, s in slot_w:
        link.arrived(ref, s)
    term[...] = gw2[0] + gw2[1] + gw2[2] + gw2[3]
    for db in (0, 1, -1, 2):
        for h in (0, 1):
            got = spot(h, 2, db, p)
            link.arrived(got, slots[h, "t", db])
            hand(got, spot(h, 2, db, 1 - p))
    for ref, s in twins:
        link.arrived(ref, s)
    link.drain()


def scatter_z(part, term, out, gw, summed, inbox, wz, wfull, send, recv):
    r, c, p = lax.axis_index("row"), lax.axis_index("col"), lax.axis_index("rep")
    n = part.shape[0]
    x, y = c // SIDE, lax.rem(c, SIDE)
    wrap = lambda v: lax.rem(v + 2 * SIDE, SIDE)
    at = lambda k: lax.rem(r + k + 2 * n, n)
    right, left, twin = {"row": at(1)}, {"row": at(-1)}, {"rep": 1 - p}
    column = [{"row": at(k)} for k in range(1, n)]
    mates = [{"col": x * SIDE + wrap(y + k)} for k in range(1, SIDE)]
    peers = [{"col": wrap(x + k) * SIDE + y, "rep": lax.rem(p + e, 2)}
             for k in range(SIDE) for e in range(2) if (k, e) != (0, 0)]
    enter([*column, *mates, *peers])
    link = Link(send, recv)
    half = n // 2
    order = [half, *[s * k for k in range(half - 1, 0, -1) for s in (1, -1)], 0]
    cores = {}
    for k in order:
        cores[k] = link.slot()
        link.start(part.at[at(k), 1 - p], summed.at[at(k)], twin, cores[k])
    wait_w = []
    for k in range(1, n):
        s = link.slot()
        link.start(term, wz.at[r], {"row": at(k)}, s)
        wait_w.append((wz.at[at(-k)], s))
    wz[r] = term[...]

    def merge(k):
        link.arrived(summed.at[at(k)], cores[k])
        summed[at(k)] = add(summed[at(k)], part[at(k), p])

    subs = 4
    rows = summed.shape[1] // subs
    span = lambda j: pl.ds(j * rows, rows)
    slots = {}

    def go(k, d, j):
        dev = right if d == 1 else left
        slots[k, d, j] = link.slot()
        link.start(summed.at[at(k * d), span(j)], inbox.at[k - 1, (1 - d) // 2, span(j)], dev, slots[k, d, j])

    def far_part(d, j):
        return (j < subs // 2) == (d == 1)

    merge(half)
    for j in range(subs):
        for d in (1, -1):
            if far_part(d, j):
                go(half, d, j)
    eighth = term.shape[0]
    share = eighth * SIDE
    mine8 = x * 2 + p
    for k in range(half - 1, 0, -1):
        merge(k)
        merge(-k)
        for j in range(subs):
            for d in (1, -1):
                if k == half - 1 and not far_part(d, j):
                    go(k, d, j)
        for j in range(subs):
            for d in (1, -1):
                if k == half - 1 and not far_part(d, j):
                    continue
                link.arrived(inbox.at[k, (1 - d) // 2, span(j)], slots[k + 1, d, j])
                piece = summed.at[at(k * d), span(j)]
                piece[...] = add(piece[...], inbox[k, (1 - d) // 2, span(j)])
                go(k, d, j)
        if k == half - 1:
            for ref, s in wait_w:
                link.arrived(ref, s)
            total = wz[0]
            for i in range(1, n):
                total += wz[i]
            mine = wfull.at[pl.ds(mine8 * share + y * eighth, eighth)]
            mine[...] = total
            wait_w = []
            for k2 in range(1, SIDE):
                s = link.slot()
                link.start(mine, mine, {"col": x * SIDE + wrap(y + k2)}, s)
                wait_w.append((wfull.at[pl.ds(mine8 * share + wrap(y - k2) * eighth, eighth)], s))
        if k == half - 2:
            for ref, s in wait_w:
                link.arrived(ref, s)
            wait_w = []
            mine = wfull.at[pl.ds(mine8 * share, share)]
            for k2 in range(SIDE):
                for e in range(2):
                    if (k2, e) == (0, 0):
                        continue
                    core = lax.rem(p + e, 2)
                    s = link.slot()
                    link.start(mine, mine, {"col": wrap(x + k2) * SIDE + y, "rep": core}, s)
                    there = wrap(x - k2) * 2 + core
                    wait_w.append((wfull.at[pl.ds(there * share, share)], s))
    merge(0)
    for ref, s in wait_w:
        link.arrived(ref, s)
    gw[...] = wfull[:, : gw.shape[1]]
    for j in range(subs):
        for d in (1, -1):
            link.arrived(inbox.at[0, (1 - d) // 2, span(j)], slots[1, d, j])
        out[span(j)] = (
            summed[r, span(j)].astype(F32)
            + inbox[0, 0, span(j)].astype(F32)
            + inbox[0, 1, span(j)].astype(F32)
        )
    link.drain()


def call(kernel, outs, scratch, copies, number, *args):
    return pl.pallas_call(
        kernel,
        out_shape=[jax.ShapeDtypeStruct(s, t) for s, t in outs],
        in_specs=[pl.BlockSpec(memory_space=VM)] * len(args),
        out_specs=[pl.BlockSpec(memory_space=VM)] * len(outs),
        scratch_shapes=[
            *[VM(s, t) for s, t in scratch],
            pltpu.SemaphoreType.DMA((copies,)),
            pltpu.SemaphoreType.DMA((copies,)),
        ],
        compiler_params=pltpu.CompilerParams(
            collective_id=number, has_side_effects=True, vmem_limit_bytes=48 * 1024 * 1024
        ),
    )(*args)


def do_gather_z(features, n_row, n_rep):
    rows, width = features.shape
    return call(gather_z, [((n_row, n_rep, rows, width), BF)], [], 40, 0, features)[0]


def do_plane(part, weight, labels):
    side, _, _, rows, width = part.shape
    classes = weight.shape[1]
    lanes = 256
    half = rows // 2
    share = width // (2 * SIDE)
    return call(
        plane_kernel,
        [((rows, classes), F32), (part.shape, BF), ((share // SIDE, lanes), F32)],
        [
            ((side, side, rows, width), BF),
            ((2, 2, side // 2, half, width), BF),
            ((2, 2, side, half, width), BF),
            ((2, side, half, width), BF),
            ((2, 2, half // 2, width), BF),
            ((2, 2, half, width), BF),
            ((rows, width), BF),
            ((width, lanes), BF),
            ((width, lanes), F32),
            ((2 * SIDE, share, lanes), F32),
            ((SIDE, share // SIDE, lanes), F32),
        ],
        140,
        1,
        part,
        weight,
        labels,
    )


def do_scatter_z(part, term, classes):
    n, _, rows, width = part.shape
    lanes = term.shape[1]
    return call(
        scatter_z,
        [((rows, width), F32), ((width, classes), F32)],
        [
            ((n, rows, width), BF),
            ((n // 2, 2, rows, width), BF),
            ((n, *term.shape), F32),
            ((width, lanes), F32),
        ],
        90,
        2,
        part,
        term,
    )


def local(features, tile_values, tile_row, tile_col, tile_count, weight, labels):
    tile = tile_values.shape[-1]
    slots = tile_values.shape[3]
    rows, width = features.shape
    classes = weight.shape[1]
    n_row = lax.axis_size("row")
    n_col = lax.axis_size("col")
    n_rep = lax.axis_size("rep")
    row_blocks = n_col * n_rep * rows // tile
    col_blocks = n_row * n_rep * rows // tile
    values = tile_values.reshape(slots, tile, tile)
    block_rows = tile_row.reshape(slots)
    block_cols = tile_col.reshape(slots)
    count = tile_count.reshape(1)
    panel = do_gather_z(features, n_row, n_rep).reshape(col_blocks, tile, width)
    part = multiply(False, values, block_cols, block_rows, count, panel, row_blocks)
    part = part.reshape(SIDE, SIDE, n_rep, rows, width)
    logits, row_panel, term = do_plane(part, weight, labels.reshape(1, rows))
    row_panel = row_panel.reshape(row_blocks, tile, width)
    back = multiply(True, values, block_rows, block_cols, count, row_panel, col_blocks)
    back = back.reshape(n_row, n_rep, rows, width)
    grad_features, grad_weight = do_scatter_z(back, term, classes)
    return (logits, grad_features, grad_weight)


def solution(mesh):
    in_specs = (
        P(("row", "col", "rep"), None),
        P("row", "col", "rep", None, None, None),
        P("row", "col", "rep", None),
        P("row", "col", "rep", None),
        P("row", "col", "rep"),
        P(),
        P(("row", "col", "rep")),
    )
    out_specs = (P(("row", "col", "rep"), None), P(("row", "col", "rep"), None), P())
    return jax.shard_map(local, mesh=mesh, in_specs=in_specs, out_specs=out_specs, check_vma=False)
```

time: 637 us -> 135 us (0.21)
  waiting for transfers between devices: 462 us -> 0 us
  Pallas kernels: 0 us -> 125 us
  other arithmetic: 86.3 us -> 0 us
  matrix products: 34.8 us -> 0 us
  local copies, waits for them, and re-layouts: 37.7 us -> 7.45 us
  between operations: 14.5 us -> 1.35 us
    reduce_scatter x2 -> x0, waiting for transfers between devices: 197 us -> none  [the longest x1 133 us: local(): lax.psum_scatter(partial_value.reshape(row_blocks * tile, width), ('col',...]
    psum x1 -> x0, waiting for transfers between devices: 178 us -> none  [local(): lax.psum(jnp.dot(hidden.T, grad_logits, preferred_element_type=jnp.float3...]
    pallas_call x0 -> x5, Pallas kernels: none -> 125 us  [the longest x3 92.2 us: call(): pl.pallas_call(kernel, out_shape=[jax.ShapeDtypeStruct(s, t) for s, t in...]
    all_gather x2 -> x0, waiting for transfers between devices: 86 us -> none  [the longest x1 43.9 us: local(): lax.all_gather(features, ('row', 'rep'), axis=0, tiled=True)]
    scatter-add x8 -> x0, other arithmetic: 79.9 us -> none  [step(): return total.at[put].add(prod)]
    dot_general x11 -> x0, matrix products: 34.8 us -> none  [the longest x4 16 us: step(): jnp.einsum('gji,gjw->giw', part, picked, preferred_element_type=jnp.float32)]
    gather x8 -> x0, local copies, waits for them, and re-layouts: 20.6 us -> none  [step(): picked = jnp.take(source, take, axis=0)]
    broadcast_in_dim x2 -> x0, local copies, waits for them, and re-layouts: 6.8 us -> none  [the longest x1 4.26 us: local(): partial_value = jnp.zeros((row_blocks, tile, width), jnp.float32)]
  transfers between devices with their start and end apart: 5 -> 0, of which waited for: 5 -> 0; matrix products, arithmetic and copies ran while one was open for 13% -> 0% of each run, Pallas kernels for 0% -> 0%
where the time goes in v1:
time: 135 us; the launch traced here: 134 us
  Pallas kernels  125 us (93%)
  local copies, waits for them, and re-layouts  7.45 us (6%)
  between operations  1.35 us (1%)
    pallas_call x3, Pallas kernels, call(): pl.pallas_call(kernel, out_shape=[jax.ShapeDtypeStruct(s, t) for s, t in...  92.2 us
    pallas_call x2, Pallas kernels, multiply(): pl.pallas_call(functools.partial(tiles_kernel, backward), out_shape=jax.S...  32.7 us
    unnamed x18, local copies, waits for them, and re-layouts  7.45 us

profile of v1, /device:TPU:8, one launch (start us, length us, event | category | flops | bytes accessed | tf_op | source)
XLA Modules:
  0.0 133.8 jit_solution(14600798888981637920)
XLA Ops:
  1.3 1.0 copy.10.weight
  2.3 0.0 copy-start.1
  2.3 0.9 copy-done.1
  3.2 23.1 %shard_map.94 = bf16[8,2,256,256]{3,2,1,0:T(8,128)(2,1)S(1)} custom-call(bf16[256,256]{1,0:T(8,128)(2,1)S(1)} %copy-done.1), custom_call_target="tpu_custom_call" | custom-call | tf_op jit(solution)/shard_map/pallas_call | solution.py:479
  26.3 0.0 copy-start.2
  26.3 0.7 copy-done.2
  27.0 0.0 copy-start.4
  27.0 0.7 copy-done.4
  27.7 0.0 copy-start.6
  27.7 16.4 %shard_map.95 = bf16[64,128,256]{2,1,0:T(8,128)(2,1)} custom-call(s32[192]{0:T(256)S(1)} %bitcast.14, s32[192]{0:T(256)S(1)} %bitcast.16, s32[1]{0:T(128)} %bitcast.9.count, bf16[192,128,128]{2,1,0:T(8,128)(2,1)} %bitcast.19, bf16[32,128,256]{2,1,0:T(8,128)(2,1)S(1)} %bitcast.12), custom_call_target="tpu_custom_call" | custom-call | tf_op jit(solution)/shard_map/pallas_call | solution.py:133
  44.0 0.0 copy-start.3
  44.1 0.0 copy-start.5
  44.1 0.0 copy-done.6
  44.1 46.0 %shard_map.96 = (f32[256,172]{1,0:T(8,128)S(1)}, bf16[4,4,2,256,256]{4,3,2,1,0:T(8,128)(2,1)S(1)}, f32[8,256]{1,0:T(8,128)S(1)}) custom-call(bf16[4,4,2,256,256]{4,3,2,1,0:T(8,128)(2,1)} %bitcast.21, bf16[256,172]{1,0:T(8,128)(2,1)S(1)} %copy.10.weight, s32[1,256]{1,0:T(1,128)S(1)} %bitcast.18), custom_call_target="tpu_custom_call" | custom-call | tf_op jit(solution)/shard_map/pallas_call | solution.py:479
  90.1 0.0 copy-start
  90.1 1.9 %copy-done = bf16[4,4,2,256,256]{4,3,2,1,0:T(8,128)(2,1)} copy-done((bf16[4,4,2,256,256]{4,3,2,1,0:T(8,128)(2,1)}, bf16[4,4,2,256,256]{4,3,2,1,0:T(8,128)(2,1)S(1)}, u32[]{:S(2)}) %copy-start) | copy-done | bytes 4194328
  92.0 0.8 copy.11
  92.8 0.0 copy-done.3
  92.8 0.0 copy-done.5
  92.8 16.4 %shard_map.97 = bf16[32,128,256]{2,1,0:T(8,128)(2,1)S(1)} custom-call(s32[192]{0:T(256)S(1)} %bitcast.17, s32[192]{0:T(256)S(1)} %bitcast.15, s32[1]{0:T(128)} %bitcast.10.count, bf16[192,128,128]{2,1,0:T(8,128)(2,1)} %bitcast.20, bf16[64,128,256]{2,1,0:T(8,128)(2,1)} %bitcast.13), custom_call_target="tpu_custom_call" | custom-call | tf_op jit(solution)/shard_map/pallas_call | solution.py:133
  109.2 23.1 %shard_map.98 = (f32[256,256]{1,0:T(8,128)S(1)}, f32[256,172]{1,0:T(8,128)S(1)}) custom-call(bf16[8,2,256,256]{3,2,1,0:T(8,128)(2,1)S(1)} %bitcast.11, f32[8,256]{1,0:T(8,128)S(1)} %get-tuple-element.10.term), custom_call_target="tpu_custom_call" | custom-call | tf_op jit(solution)/shard_map/pallas_call | solution.py:479
  132.3 0.8 copy.12
  133.1 0.7 copy.15
Async XLA Ops:
  2.3 0.9 copy-start.1
  26.3 0.7 copy-start.2
  27.0 0.7 copy-start.4
  27.7 16.4 %copy-start.6 = (s32[256]{0:T(256)S(1)}, s32[256]{0:T(256)}, u32[]{:S(2)}) copy-start(s32[256]{0:T(256)} %param.13) | copy-start | bytes 3076
  44.0 48.8 %copy-start.3 = (s32[1,1,1,192]{3,2,1,0:T(1,128)S(1)}, s32[1,1,1,192]{3,2,1,0:T(1,128)}, u32[]{:S(2)}) copy-start(s32[1,1,1,192]{3,2,1,0:T(1,128)} %param.10) | copy-start | bytes 2308
  44.1 48.8 %copy-start.5 = (s32[1,1,1,192]{3,2,1,0:T(1,128)S(1)}, s32[1,1,1,192]{3,2,1,0:T(1,128)}, u32[]{:S(2)}) copy-start(s32[1,1,1,192]{3,2,1,0:T(1,128)} %param.9) | copy-start | bytes 2308
  90.1 1.9 %copy-start = (bf16[4,4,2,256,256]{4,3,2,1,0:T(8,128)(2,1)}, bf16[4,4,2,256,256]{4,3,2,1,0:T(8,128)(2,1)S(1)}, u32[]{:S(2)}) copy-start(bf16[4,4,2,256,256]{4,3,2,1,0:T(8,128)(2,1)S(1)} %get-tuple-element.9) | copy-start | bytes 12582916
